TPU v7x, 768 devices: a whole 4x8x12 slice. The times are simulated.
768 devices in a mesh: dp: 96 (over z, x, core), table: 8 (over y).
Axes of the slice: x: 4, y: 8, z: 12, core: 2. Of those that a mesh axis runs over, the one named last changes fastest.
Arguments:
- hot_rows: bfloat16 [96, 8, 1024, 256], P('dp', 'table'), may hold values from -6 to 6
- hot_index: int32 [96, 8, 2048], P('dp', 'table'), may hold values from 0 to 1023
- hot_bag: int32 [96, 8, 2048], P('dp', 'table'), may hold values from 0 to 1023, never falling along the last dimension, each value on 1 to 4 neighbouring positions
- cold_rows: bfloat16 [96, 8, 1024, 128], P('dp', 'table'), may hold values from -6 to 6
- cold_index: int32 [96, 8, 2048], P('dp', 'table'), may hold values from 0 to 1023
- cold_bag: int32 [96, 8, 2048], P('dp', 'table'), may hold values from 0 to 1023, never falling along the last dimension, each value on 1 to 4 neighbouring positions
- hot_proj: bfloat16 [8, 256, 512], P('table'), may hold values from -0.375 to 0.375
- cold_proj: bfloat16 [8, 128, 512], P('table'), may hold values from -0.5 to 0.5
- cotangent: float32 [98304, 256], P(('dp', 'table')), may hold values from -6 to 6
Outputs:
- interaction: float32 [98304, 256], P(('dp', 'table'))
- grad_hot_proj: float32 [8, 256, 512], P('table')
- grad_cold_proj: float32 [8, 128, 512], P('table')
- grad_hot_rows: float32 [96, 8, 1024, 256], P('dp', 'table')
- grad_cold_rows: float32 [96, 8, 1024, 128], P('dp', 'table')
Inputs may be any that keep to these rules, and one draw needn't show every extreme that they name: `hot_bag`: within each data group and table the bag numbers never fall; every sample of the group has a bag of 1 to 4 lookups. `cold_bag`: within each data group and table the bag numbers never fall; every sample of the group has a bag of 1 to 4 lookups.
All inputs are finite; a program needn't handle non-finite values.
Results may differ from a plain program's by a relative error of at most 0.0059.
Values may be sent and summed in bfloat16 or wider, within the bound.
A program may use at most 32 MiB of HBM per device.

v0:
```python
import math

import jax
import jax.numpy as jnp
from jax import lax
from jax.sharding import PartitionSpec as P


def pool_bags(table_set, index_set, bag_set, groups):

    def pool_table(table_rows, table_index, table_bag):
        picked = table_rows[table_index].astype(jnp.float32)
        return jax.ops.segment_sum(picked, table_bag, num_segments=groups, indices_are_sorted=True)

    return jax.vmap(pool_table)(table_set[0], index_set[0], bag_set[0]).astype(jnp.bfloat16)


def spread_rows(back_grad, index_set, bag_set, touched):

    def spread_table(table_grad, table_index, table_bag):
        picked = table_grad[table_bag].astype(jnp.float32)
        return jax.ops.segment_sum(picked, table_index, num_segments=touched)

    return jax.vmap(spread_table)(back_grad, index_set[0], bag_set[0])[None]


def local(
    hot_rows, hot_index, hot_bag, cold_rows, cold_index, cold_bag, hot_proj, cold_proj, cotangent
):
    batch = cotangent.shape[0]
    groups = batch * lax.axis_size("table")
    touched = hot_rows.shape[2]
    hot_pooled = pool_bags(hot_rows, hot_index, hot_bag, groups)
    cold_pooled = pool_bags(cold_rows, cold_index, cold_bag, groups)
    hot_recv, cold_recv = (
        lax.all_to_all(hot_pooled, "table", split_axis=1, concat_axis=0, tiled=True),
        lax.all_to_all(cold_pooled, "table", split_axis=1, concat_axis=0, tiled=True),
    )
    hot_all, cold_all = (
        lax.all_gather(hot_proj, "table", axis=0, tiled=True),
        lax.all_gather(cold_proj, "table", axis=0, tiled=True),
    )
    hot_feat = jnp.einsum(
        "tbw,twd->tbd", hot_recv, hot_all, preferred_element_type=jnp.float32
    ).astype(jnp.bfloat16)
    cold_feat = jnp.einsum(
        "tbw,twd->tbd", cold_recv, cold_all, preferred_element_type=jnp.float32
    ).astype(jnp.bfloat16)
    features = jnp.concatenate([hot_feat, cold_feat], axis=0)
    tables = features.shape[0]
    hot_count = hot_feat.shape[0]
    root_scale = 1.0 / math.sqrt(features.shape[2])
    pair_dots = (
        jnp.einsum("tbd,ubd->btu", features, features, preferred_element_type=jnp.float32)
        * root_scale
    )
    cot_block = cotangent.reshape(batch, tables, tables)
    symmetric = cot_block + jnp.transpose(cot_block, (0, 2, 1))
    feat_wide = features.astype(jnp.float32)
    grad_feat = (
        jnp.einsum("btu,ubd->tbd", symmetric, feat_wide, precision=lax.Precision.HIGHEST)
        * root_scale
    ).astype(jnp.bfloat16)
    hot_grad, cold_grad = (
        lax.all_to_all(grad_feat[:hot_count], "table", split_axis=0, concat_axis=1, tiled=True),
        lax.all_to_all(grad_feat[hot_count:], "table", split_axis=0, concat_axis=1, tiled=True),
    )
    hot_wpart = jnp.einsum("tsw,tsd->twd", hot_pooled, hot_grad, preferred_element_type=jnp.float32)
    cold_wpart = jnp.einsum(
        "tsw,tsd->twd", cold_pooled, cold_grad, preferred_element_type=jnp.float32
    )
    hot_wsum, cold_wsum = lax.psum((hot_wpart, cold_wpart), "dp")
    replicas = lax.axis_size("dp")
    hot_back = jnp.einsum(
        "tsd,twd->tsw", hot_grad, hot_proj, preferred_element_type=jnp.float32
    ).astype(jnp.bfloat16)
    cold_back = jnp.einsum(
        "tsd,twd->tsw", cold_grad, cold_proj, preferred_element_type=jnp.float32
    ).astype(jnp.bfloat16)
    hot_grads = spread_rows(hot_back, hot_index, hot_bag, touched)
    cold_grads = spread_rows(cold_back, cold_index, cold_bag, touched)
    return (
        pair_dots.reshape(batch, tables * tables),
        hot_wsum / replicas,
        cold_wsum / replicas,
        hot_grads,
        cold_grads,
    )


def solution(mesh):
    return jax.shard_map(
        local,
        mesh=mesh,
        in_specs=(
            P("dp", "table", None, None),
            P("dp", "table", None),
            P("dp", "table", None),
            P("dp", "table", None, None),
            P("dp", "table", None),
            P("dp", "table", None),
            P("table", None, None),
            P("table", None, None),
            P(("dp", "table"), None),
        ),
        out_specs=(
            P(("dp", "table"), None),
            P("table", None, None),
            P("table", None, None),
            P("dp", "table", None, None),
            P("dp", "table", None, None),
        ),
        check_vma=False,
    )
```

profile of v0, /device:TPU:1, one launch (start us, length us, event | category | flops | bytes accessed | tf_op | source)
XLA Modules:
  0.0 470.8 jit_solution(2345630720872420573)
XLA Ops:
  11.9 26.8 %scatter_custom_fusion.1 = f32[1024,128]{1,0:T(8,128)S(1)} fusion(s32[2048]{0:T(1024)S(1)} %get-tuple-element.32, f32[]{:T(128)} %constant.5.clone.1, bf16[1,1024,128]{2,1,0:T(8,128)(2,1)} %bitcast.84, s32[2048]{0:T(1024)S(1)} %bitcast.96), kind=kCustom, calls=%fused_computation.29 | custom fusion | flops 524288 | bytes 794628
  39.7 2.2 reduce.24
  42.6 7.6 %all-to-all-start.1 = ((bf16[8,2,8192]{2,1,0:T(2,128)(2,1)}), bf16[8,2,8192]{2,1,0:T(2,128)(2,1)S(1)}, u32[]{:S(2)}, u32[]{:S(2)}) async-start(bf16[8,2,8192]{2,1,0:T(2,128)(2,1)} %reshape.408), calls=%async_computation.1 | async-start | bytes 524288 | tf_op jit(solution)/shard_map/all_to_all | solution.py:37
  50.3 19.1 %scatter_custom_fusion = f32[1024,256]{1,0:T(8,128)S(1)} fusion(s32[2048]{0:T(1024)S(1)} %get-tuple-element.33, f32[]{:T(128)} %constant.5.clone.1, bf16[1,1024,256]{2,1,0:T(8,128)(2,1)S(1)} %bitcast.69, s32[2048]{0:T(1024)S(1)} %bitcast.95), kind=kCustom, calls=%fused_computation.12 | custom fusion | flops 1048576 | bytes 1581060
  70.3 4.7 reduce.25
  75.0 2.0 reshape.410
  77.0 6.6 %all-to-all-start = ((bf16[8,2,16384]{2,1,0:T(2,128)(2,1)}), bf16[8,2,16384]{2,1,0:T(2,128)(2,1)}, u32[]{:S(2)}, u32[]{:S(2)}) async-start(bf16[8,2,16384]{2,1,0:T(2,128)(2,1)} %reshape.410), calls=%async_computation | async-start | bytes 1048576 | tf_op jit(solution)/shard_map/all_to_all | solution.py:36
  84.6 19.9 %all-to-all-done = bf16[8,2,16384]{2,1,0:T(2,128)(2,1)} async-done(((bf16[8,2,16384]{2,1,0:T(2,128)(2,1)}), bf16[8,2,16384]{2,1,0:T(2,128)(2,1)}, u32[]{:S(2)}, u32[]{:S(2)}) %all-to-all-start) | async-done | bytes 524320 | tf_op jit(solution)/shard_map/all_to_all | solution.py:36
  104.5 2.2 reshape.411
  107.6 1.7 convolution_convert_fusion.1
  109.2 7.6 %all-gather.3.cloned.1.call-done = bf16[8,256,512]{2,1,0:T(8,128)(2,1)} async-done(((bf16[1,256,512]{2,1,0:T(8,128)(2,1)}), bf16[8,256,512]{2,1,0:T(8,128)(2,1)}) %all-gather.3.cloned.1.call-update) | async-done | bytes 2097168 | tf_op jit(solution)/shard_map/all_gather | solution.py:40
  116.9 2.2 convolution_convert_fusion
  119.3 2.7 fusion.7
  123.5 4.2 all-to-all-start.2
  129.0 25.7 %all-to-all-done.2 = bf16[8,128,512]{2,1,0:T(8,128)(2,1)S(1)} async-done(((bf16[8,128,512]{2,1,0:T(8,128)(2,1)}), bf16[8,128,512]{2,1,0:T(8,128)(2,1)S(1)}, u32[]{:S(2)}, u32[]{:S(2)}) %all-to-all-start.2) | async-done | bytes 1048608 | tf_op jit(solution)/shard_map/all_to_all | solution.py:65
  154.7 3.6 all-to-all-start.3
  159.8 2.5 convolution_bitcast_fusion
  162.3 23.1 %all-to-all-done.3 = bf16[8,128,512]{2,1,0:T(8,128)(2,1)S(1)} async-done(((bf16[8,128,512]{2,1,0:T(8,128)(2,1)}), bf16[8,128,512]{2,1,0:T(8,128)(2,1)S(1)}, u32[]{:S(2)}, u32[]{:S(2)}) %all-to-all-start.3) | async-done | bytes 1048608 | tf_op jit(solution)/shard_map/all_to_all | solution.py:66
  186.4 5.6 %fusion.10 = f32[128,16,16]{2,1,0:T(8,128)} fusion(bf16[16,128,512]{2,1,0:T(8,128)(2,1)} %copy-done.2), kind=kOutput, calls=%fused_computation.20 | convolution fusion | flops 33587200 | bytes 2228224 | tf_op jit(solution)/shard_map/tbd,ubd->btu/dot_general | solution.py:54
  194.9 19.7 %scatter_custom_fusion.2 = f32[1024,256]{1,0:T(8,128)} fusion(s32[2048]{0:T(1024)} %broadcast_select_fusion.1, f32[]{:T(128)} %constant.5.clone.1, bf16[1,1024,256]{2,1,0:T(8,128)(2,1)S(1)} %fusion.13, s32[2048]{0:T(1024)S(1)} %bitcast.94), kind=kCustom, calls=%fused_computation.10 | custom fusion | flops 1048576 | bytes 1581568
  215.1 18.3 %scatter_custom_fusion.3 = f32[1024,128]{1,0:T(8,128)} fusion(s32[2048]{0:T(1024)} %broadcast_select_fusion, f32[]{:T(128)} %constant.5.clone.1, bf16[1,1024,128]{2,1,0:T(8,128)(2,1)S(1)} %fusion.14, s32[2048]{0:T(1024)S(1)} %bitcast.93), kind=kCustom, calls=%fused_computation.27 | custom fusion | flops 524288 | bytes 795136
  233.4 227.3 %all-reduce.3.cloned.1.call-done = (f32[1,256,512]{2,1,0:T(8,128)}, f32[1,128,512]{2,1,0:T(8,128)}) async-done(((f32[1,256,512]{2,1,0:T(8,128)}, f32[1,128,512]{2,1,0:T(8,128)}), (f32[1,256,512]{2,1,0:T(8,128)}, f32[1,128,512]{2,1,0:T(8,128)})) %all-reduce.3.cloned.1.call-update) | async-done | bytes 786448 | tf_op jit(solution)/shard_map/psum | solution.py:72
  460.7 1.9 broadcast_multiply_fusion
  462.6 1.7 broadcast_multiply_fusion.1
  (68 shorter events, 18.0 us)
Async XLA Ops:
  7.2 43.2 %copy-start = (bf16[1,1,1024,256]{3,2,1,0:T(8,128)(2,1)S(1)}, bf16[1,1,1024,256]{3,2,1,0:T(8,128)(2,1)}, u32[]{:S(2)}) copy-start(bf16[1,1,1024,256]{3,2,1,0:T(8,128)(2,1)} %param.9) | copy-start | bytes 1572868
  7.2 100.4 %all-gather.5.cloned.1.call-start = ((), (), s32[]{:S(2)}) async-start(), calls=%async_computation.5 | async-start | bytes 1179648 | tf_op jit(solution)/shard_map/all_gather | solution.py:41
  7.9 108.9 %all-gather.3.cloned.1.call-start = ((), (), s32[]{:S(2)}) async-start(), calls=%async_computation.4 | async-start | bytes 2359296 | tf_op jit(solution)/shard_map/all_gather | solution.py:40
  11.9 38.4 %copy-start.6 = (s32[1,1,2048]{2,1,0:T(1,128)S(1)}, s32[1,1,2048]{2,1,0:T(1,128)}, u32[]{:S(2)}) copy-start(s32[1,1,2048]{2,1,0:T(1,128)} %param.10) | copy-start | bytes 24580
  42.6 34.3 %all-to-all-start.1 = ((bf16[8,2,8192]{2,1,0:T(2,128)(2,1)}), bf16[8,2,8192]{2,1,0:T(2,128)(2,1)S(1)}, u32[]{:S(2)}, u32[]{:S(2)}) async-start(bf16[8,2,8192]{2,1,0:T(2,128)(2,1)} %reshape.408), calls=%async_computation.1 | async-start | bytes 524288 | tf_op jit(solution)/shard_map/all_to_all | solution.py:37
  69.4 5.6 %copy-start.1 = (f32[1024,256]{1,0:T(8,128)}, f32[1024,256]{1,0:T(8,128)S(1)}, u32[]{:S(2)}) copy-start(f32[1024,256]{1,0:T(8,128)S(1)} %scatter_custom_fusion) | copy-start | bytes 3145732
  70.3 13.3 %copy-start.5 = (f32[128,256]{1,0:T(8,128)S(1)}, f32[128,256]{1,0:T(8,128)}, u32[]{:S(2)}) copy-start(f32[128,256]{1,0:T(8,128)} %param.17) | copy-start | bytes 393220
  77.0 27.5 %all-to-all-start = ((bf16[8,2,16384]{2,1,0:T(2,128)(2,1)}), bf16[8,2,16384]{2,1,0:T(2,128)(2,1)}, u32[]{:S(2)}, u32[]{:S(2)}) async-start(bf16[8,2,16384]{2,1,0:T(2,128)(2,1)} %reshape.410), calls=%async_computation | async-start | bytes 1048576 | tf_op jit(solution)/shard_map/all_to_all | solution.py:36
  119.3 2.7 copy-start.2
  122.2 5.5 %copy-start.7 = (s32[1,1,2048]{2,1,0:T(1,128)S(1)}, s32[1,1,2048]{2,1,0:T(1,128)}, u32[]{:S(2)}) copy-start(s32[1,1,2048]{2,1,0:T(1,128)} %param.11) | copy-start | bytes 24580
  122.2 5.5 %copy-start.8 = (s32[1,1,2048]{2,1,0:T(1,128)S(1)}, s32[1,1,2048]{2,1,0:T(1,128)}, u32[]{:S(2)}) copy-start(s32[1,1,2048]{2,1,0:T(1,128)} %param.14) | copy-start | bytes 24580
  123.5 31.2 %all-to-all-start.2 = ((bf16[8,128,512]{2,1,0:T(8,128)(2,1)}), bf16[8,128,512]{2,1,0:T(8,128)(2,1)S(1)}, u32[]{:S(2)}, u32[]{:S(2)}) async-start(bf16[8,128,512]{2,1,0:T(8,128)(2,1)} %copy.47), calls=%async_computation.2 | async-start | bytes 2097152 | tf_op jit(solution)/shard_map/all_to_all | solution.py:65
  127.7 30.9 %copy-start.10 = (pred[2048]{0:T(1024)(128)(4,1)S(1)}, pred[2048]{0:T(1024)(128)(4,1)}, u32[]{:S(2)}) copy-start(pred[2048]{0:T(1024)(128)(4,1)} %get-tuple-element.26) | copy-start | bytes 6148
  127.7 31.5 %copy-start.9 = (pred[2048]{0:T(1024)(128)(4,1)S(1)}, pred[2048]{0:T(1024)(128)(4,1)}, u32[]{:S(2)}) copy-start(pred[2048]{0:T(1024)(128)(4,1)} %get-tuple-element.24) | copy-start | bytes 6148
  154.7 30.7 %all-to-all-start.3 = ((bf16[8,128,512]{2,1,0:T(8,128)(2,1)}), bf16[8,128,512]{2,1,0:T(8,128)(2,1)S(1)}, u32[]{:S(2)}, u32[]{:S(2)}) async-start(bf16[8,128,512]{2,1,0:T(8,128)(2,1)} %copy.48), calls=%async_computation.3 | async-start | bytes 2097152 | tf_op jit(solution)/shard_map/all_to_all | solution.py:66
  158.2 302.5 %all-reduce.3.cloned.1.call-start = ((), (), s32[]{:S(2)}) async-start(), calls=%async_computation.6 | async-start | bytes 1572864 | tf_op jit(solution)/shard_map/psum | solution.py:72
  186.4 8.0 %copy-start.3 = (bf16[1,256,512]{2,1,0:T(8,128)(2,1)S(1)}, bf16[1,256,512]{2,1,0:T(8,128)(2,1)}, u32[]{:S(2)}) copy-start(bf16[1,256,512]{2,1,0:T(8,128)(2,1)} %param.15) | copy-start | bytes 786436
  193.6 21.0 %copy-start.4 = (bf16[1,128,512]{2,1,0:T(8,128)(2,1)S(1)}, bf16[1,128,512]{2,1,0:T(8,128)(2,1)}, u32[]{:S(2)}) copy-start(bf16[1,128,512]{2,1,0:T(8,128)(2,1)} %param.16) | copy-start | bytes 393220
Sparse Core Ops, SparseCore 0:
  10.4 47.4 all-gather.4
  60.3 56.5 all-gather.2
  186.5 274.1 all-reduce.2
where the time goes:
time: 472 us; the launch traced here: 471 us
  waiting for transfers between devices  305 us (65%)
  other arithmetic  99.2 us (21%)
  starting transfers between devices  22.3 us (5%)
  matrix products  16.6 us (4%)
  between operations  14.1 us (3%)
  local copies, waits for them, and re-layouts  13.7 us (3%)
    psum x1, waiting for transfers between devices, local(): hot_wsum, cold_wsum = lax.psum((hot_wpart, cold_wpart), 'dp')  227 us
    unnamed x11, other arithmetic  94.5 us
    all_to_all x1, waiting for transfers between devices, local(): lax.all_to_all(grad_feat[:hot_count], 'table', split_axis=0, concat_axis=...  25.7 us
    all_to_all x1, waiting for transfers between devices, local(): lax.all_to_all(grad_feat[hot_count:], 'table', split_axis=0, concat_axis=...  23.1 us
    all_to_all x1, waiting for transfers between devices, local(): lax.all_to_all(hot_pooled, 'table', split_axis=1, concat_axis=0, tiled=True)  19.9 us
  transfers between devices with their start and end apart: 7, of which 5 were waited for; matrix products, arithmetic and copies ran while one was open for 25% of the time, Pallas kernels for 0%

commit v1 on v0

v1 whole, which is shorter than its diff:
```python
import math

import jax
import jax.numpy as jnp
from jax import lax
from jax.experimental import pallas as pl
from jax.experimental.pallas import tpu as pltpu
from jax.sharding import PartitionSpec as P

F32 = jnp.float32
BF16 = jnp.bfloat16
MESH = pl.DeviceIdType.MESH
NY = 8
NX = 4
NZ = 12
WH, WC, D = 256, 128, 512
SB = 128
GB = 1024
LOOK = 2048
ROWS = 1024
BAND = 1152
VMEM_LIMIT = 48 * 1024 * 1024


def place():
    dp = lax.axis_index("dp")
    y = lax.axis_index("table")
    core = lax.rem(dp, 2)
    x = lax.rem(lax.div(dp, 2), NX)
    z = lax.div(dp, 2 * NX)
    return dp, y, z, x, core


def dot(a, b):
    return jnp.dot(a, b, preferred_element_type=F32)


def dot_nt(a, b):
    return lax.dot_general(a, b, (((1,), (1,)), ((), ())), preferred_element_type=F32)


def dot_tn(a, b):
    return lax.dot_general(a, b, (((0,), (0,)), ((), ())), preferred_element_type=F32)


def iota(shape, dim):
    return lax.broadcasted_iota(jnp.int32, shape, dim)


def split2(v):
    hi = v.astype(BF16)
    return hi, (v - hi.astype(F32)).astype(BF16)


def main_kernel(
    hot_rows, hot_index, hot_bag, cold_rows, cold_index, cold_bag, hot_proj, cold_proj, cot,
    inter, hot_grads, cold_grads, wpart,
    hot_picked, cold_picked, hot_send, cold_send, hot_recv, cold_recv,
    hot_w, cold_w, one_index, hot_at, cold_at, m_hi, m_lo, feat, grad,
    hot_bsend, cold_bsend, hot_back, cold_back,
    pool_sem, proj_sem, x_sem, core_sem, back_sem,
):
    dp, y, z, x, core = place()
    q = core * NX + x
    right = lax.rem(x + 1, NX)
    left = lax.rem(x + NX - 1, NX)
    far = lax.rem(x + 2, NX)

    def at_x(other):
        return ((z * NX + other) * 2 + core, y)

    sibling = (dp + 1 - 2 * core, y)

    barrier = pltpu.get_barrier_semaphore()
    for d in range(1, NY):
        pl.semaphore_signal(barrier, inc=1, device_id=(dp, lax.rem(y + d, NY)), device_id_type=MESH)
    for peer in (at_x(right), at_x(left), sibling):
        pl.semaphore_signal(barrier, inc=1, device_id=peer, device_id_type=MESH)
    pl.semaphore_wait(barrier, NY - 1 + 3)

    def hslice(block):
        return pl.ds(pl.multiple_of(block * 32, 32), 32)

    def cslice(block):
        return pl.ds(pl.multiple_of(block * 16, 16), 16)

    def proj_copies(d):
        peer = (dp, lax.rem(y + d, NY))
        return (
            pltpu.make_async_remote_copy(
                src_ref=hot_proj.at[0, hslice(q)], dst_ref=hot_w.at[y, hslice(q)],
                send_sem=proj_sem.at[0, d], recv_sem=proj_sem.at[1, d],
                device_id=peer, device_id_type=MESH),
            pltpu.make_async_remote_copy(
                src_ref=cold_proj.at[0, cslice(q)], dst_ref=cold_w.at[y, cslice(q)],
                send_sem=proj_sem.at[2, d], recv_sem=proj_sem.at[3, d],
                device_id=peer, device_id_type=MESH),
        )

    def start_proj(d, c):
        for copy in proj_copies(d):
            copy.start()
        return c

    lax.fori_loop(1, NY, start_proj, 0)
    hot_w[y, hslice(q)] = hot_proj[0, hslice(q)]
    cold_w[y, cslice(q)] = cold_proj[0, cslice(q)]

    lane = iota((128, 128), 1)

    def pick(index, rows, picked):
        def chunk(k, c):
            span = pl.ds(pl.multiple_of(k * 128, 128), 128)
            own = jnp.broadcast_to(index[0, :, span], (128, 128)).T
            hit = jnp.concatenate([(own == lane + 128 * r).astype(F32).astype(BF16) for r in range(8)], axis=1)
            picked[span, :] = dot(hit, rows[0, 0]).astype(BF16)
            return c

        lax.fori_loop(0, LOOK // 128, chunk, 0)

    def bag_hits(bag, block, samples, width):
        band = pl.ds(pl.multiple_of(block * SB, SB), width)
        ids = iota((samples, width), 0) + block * SB
        return band, (bag[0, :, band] == ids).astype(F32).astype(BF16)

    def pool_copy(which, d):
        send, recv = ((hot_send, hot_recv), (cold_send, cold_recv))[which]
        peer = lax.rem(y + d, NY)
        return pltpu.make_async_remote_copy(
            src_ref=send.at[peer], dst_ref=recv.at[y],
            send_sem=pool_sem.at[2 * which, d], recv_sem=pool_sem.at[2 * which + 1, d],
            device_id=(dp, peer), device_id_type=MESH)

    def pool(which, bag, picked):
        send, recv = ((hot_send, hot_recv), (cold_send, cold_recv))[which]

        def block(d, c):
            peer = lax.rem(y + d, NY)
            band, hits = bag_hits(bag, peer, SB, BAND)
            send[peer] = dot(hits, picked[band, :]).astype(BF16)
            pool_copy(which, d).start()
            return c

        lax.fori_loop(1, NY, block, 0)
        band, hits = bag_hits(bag, y, SB, BAND)
        recv[y] = dot(hits, picked[band, :]).astype(BF16)

    pick(hot_index, hot_rows, hot_picked)
    pool(0, hot_bag, hot_picked)
    pick(cold_index, cold_rows, cold_picked)
    pool(1, cold_bag, cold_picked)

    def x_copies(slot, tables, block, peer):
        return (
            pltpu.make_async_remote_copy(
                src_ref=hot_w.at[tables, hslice(block)], dst_ref=hot_w.at[tables, hslice(block)],
                send_sem=x_sem.at[0, slot], recv_sem=x_sem.at[1, slot],
                device_id=peer, device_id_type=MESH),
            pltpu.make_async_remote_copy(
                src_ref=cold_w.at[tables, cslice(block)], dst_ref=cold_w.at[tables, cslice(block)],
                send_sem=x_sem.at[2, slot], recv_sem=x_sem.at[3, slot],
                device_id=peer, device_id_type=MESH),
        )

    def core_copies(slot, block):
        return (
            pltpu.make_async_remote_copy(
                src_ref=hot_w.at[:, hslice(block)], dst_ref=hot_w.at[:, hslice(block)],
                send_sem=core_sem.at[0, slot], recv_sem=core_sem.at[1, slot],
                device_id=sibling, device_id_type=MESH),
            pltpu.make_async_remote_copy(
                src_ref=cold_w.at[:, cslice(block)], dst_ref=cold_w.at[:, cslice(block)],
                send_sem=core_sem.at[2, slot], recv_sem=core_sem.at[3, slot],
                device_id=sibling, device_id_type=MESH),
        )

    every, low, high = pl.ds(0, NY), pl.ds(0, NY // 2), pl.ds(NY // 2, NY // 2)
    steps_x = (
        x_copies(0, every, q, at_x(right)),
        x_copies(1, every, q, at_x(left)),
        x_copies(2, low, core * NX + left, at_x(right)),
        x_copies(3, high, core * NX + right, at_x(left)),
    )
    steps_core = tuple(core_copies(n, core * NX + other) for n, other in enumerate((x, left, right, far)))

    def start(copies):
        for copy in copies:
            copy.start()

    def arrived(copies):
        for copy in copies:
            copy.wait_recv()

    def proj_arrived(d, c):
        arrived(proj_copies(d))
        return c

    lax.fori_loop(1, NY, proj_arrived, 0)
    start(steps_x[0])
    start(steps_x[1])
    start(steps_core[0])

    def counts(index, bag, out):
        def onehot(k, c):
            rows = pl.ds(pl.multiple_of(k * 128, 128), 128)
            one_index[rows, :] = (index[0] == iota((128, LOOK), 0) + k * 128).astype(F32).astype(BF16)
            return c

        lax.fori_loop(0, ROWS // 128, onehot, 0)

        def column(j, c):
            width = BAND + SB
            first = jnp.minimum(2 * j, (LOOK - width) // SB)
            band = pl.ds(pl.multiple_of(first * SB, SB), width)
            ids = iota((2 * SB, width), 0) + 2 * SB * j
            hits = (bag[0, :, band] == ids).astype(F32).astype(BF16)
            out[:, pl.ds(pl.multiple_of(j * 2 * SB, 2 * SB), 2 * SB)] = dot_nt(one_index[:, band], hits).astype(BF16)
            return c

        lax.fori_loop(0, GB // (2 * SB), column, 0)

    row = iota((256, 256), 0)
    col = iota((256, 256), 1)
    row_hi, row_lo = lax.shift_right_logical(row, 4), lax.bitwise_and(row, 15)
    col_hi, col_lo = lax.shift_right_logical(col, 4), lax.bitwise_and(col, 15)

    def ones(mask):
        return mask.astype(F32).astype(BF16)

    turn = ones((row_hi == col_lo) & (row_lo == col_hi))
    widen = ones(row_lo == col_hi)
    narrow = ones(row_hi == col_lo)
    same_hi = row_hi == col_hi
    same_lo = row_lo == col_lo

    def spread_cot(g, c):
        rows = pl.ds(pl.multiple_of(g * 16, 16), 16)
        part = cot[rows, :]
        hi, lo = split2(part)
        sym = part + (dot(hi, turn) + dot(lo, turn))
        tall = jnp.where(same_hi, jnp.concatenate([sym] * 16, axis=0), 0.0)
        hi, lo = split2(tall)
        m_hi[g] = jnp.where(same_lo, dot(hi, widen), 0.0).astype(BF16)
        m_lo[g] = jnp.where(same_lo, dot(lo, widen), 0.0).astype(BF16)
        return c

    lax.fori_loop(0, SB // 16, spread_cot, 0)
    counts(hot_index, hot_bag, hot_at)

    arrived(steps_x[0])
    start(steps_x[2])
    start(steps_core[1])
    arrived(steps_x[1])
    start(steps_x[3])
    start(steps_core[2])

    counts(cold_index, cold_bag, cold_at)

    arrived(steps_x[2])
    arrived(steps_x[3])
    start(steps_core[3])
    for copies in steps_core:
        arrived(copies)

    def pool_arrived(d, c):
        pool_copy(0, d).wait_recv()
        pool_copy(1, d).wait_recv()
        return c

    lax.fori_loop(1, NY, pool_arrived, 0)

    def features(t, c):
        feat[t] = dot(hot_recv[t], hot_w[t]).astype(BF16)
        feat[NY + t] = dot(cold_recv[t], cold_w[t]).astype(BF16)
        return c

    lax.fori_loop(0, NY, features, 0)

    root_scale = 1.0 / math.sqrt(D)

    def sixteen(g, c):
        rows = pl.ds(pl.multiple_of(g * 16, 16), 16)
        block = feat[:, rows, :].reshape(256, D)
        gram = jnp.where(same_lo, dot_nt(block, block) * root_scale, 0.0)
        hi, lo = split2(gram)
        wide = jnp.where(same_hi, dot(hi, narrow) + dot(lo, narrow), 0.0)
        inter[rows, :] = jnp.sum(wide.reshape(16, 16, 256), axis=0)
        slope = (dot(m_hi[g], block) + dot(m_lo[g], block)) * root_scale
        grad[:, rows, :] = slope.astype(BF16).reshape(16, 16, D)
        return c

    lax.fori_loop(0, SB // 16, sixteen, 0)

    def back_copy(which, d):
        send, recv = ((hot_bsend, hot_back), (cold_bsend, cold_back))[which]
        peer = lax.rem(y + d, NY)
        return pltpu.make_async_remote_copy(
            src_ref=send.at[peer], dst_ref=recv.at[y],
            send_sem=back_sem.at[2 * which, d], recv_sem=back_sem.at[2 * which + 1, d],
            device_id=(dp, peer), device_id_type=MESH)

    def hot_return(d, c):
        peer = lax.rem(y + d, NY)
        hot_bsend[peer] = dot_nt(grad[peer], hot_w[peer]).astype(BF16)
        back_copy(0, d).start()
        return c

    def cold_return(d, c):
        peer = lax.rem(y + d, NY)
        cold_bsend[peer] = dot_nt(grad[NY + peer], cold_w[peer]).astype(BF16)
        back_copy(1, d).start()
        return c

    lax.fori_loop(1, NY, hot_return, 0)
    lax.fori_loop(1, NY, cold_return, 0)
    hot_back[y] = dot_nt(grad[y], hot_w[y]).astype(BF16)
    cold_back[y] = dot_nt(grad[NY + y], cold_w[y]).astype(BF16)

    def weight_part(t, c):
        wpart[:, t, 0:32, :] = dot_tn(hot_recv[t], grad[t]).astype(BF16).reshape(8, 32, D)
        wpart[:, t, 32:48, :] = dot_tn(cold_recv[t], grad[NY + t]).astype(BF16).reshape(8, 16, D)
        return c

    lax.fori_loop(0, NY, weight_part, 0)

    def back_arrived(which):
        def one(d, c):
            back_copy(which, d).wait_recv()
            return c

        lax.fori_loop(1, NY, one, 0)

    def spread(at, back, out, width):
        def rows_of(k, c):
            rows = pl.ds(pl.multiple_of(k * 256, 256), 256)
            out[0, 0, rows, :] = dot(at[rows, :], back[...].reshape(GB, width))
            return c

        lax.fori_loop(0, ROWS // 256, rows_of, 0)

    back_arrived(0)
    spread(hot_at, hot_back, hot_grads, WH)
    back_arrived(1)
    spread(cold_at, cold_back, cold_grads, WC)

    def sent(d, c):
        for copy in proj_copies(d):
            copy.wait_send()
        for which in range(2):
            pool_copy(which, d).wait_send()
            back_copy(which, d).wait_send()
        return c

    lax.fori_loop(1, NY, sent, 0)
    for copies in steps_x + steps_core:
        for copy in copies:
            copy.wait_send()


def reduce_kernel(
    wpart, hot_out, cold_out,
    core_recv, x_send, x_recv, z_send, z_recv, y_send, y_recv, comb,
    core_sem, x_sem, z_sem, y_sem, zg_sem, xg_sem, cg_sem,
):
    dp, y, z, x, core = place()
    q = core * NX + x
    sibling = (dp + 1 - 2 * core, y)

    def at_x(d):
        return ((z * NX + lax.rem(x + d, NX)) * 2 + core, y)

    def at_z(d):
        return ((lax.rem(z + d, NZ) * NX + x) * 2 + core, y)

    barrier = pltpu.get_barrier_semaphore()
    pl.semaphore_signal(barrier, inc=1, device_id=sibling, device_id_type=MESH)
    for d in range(1, NX):
        pl.semaphore_signal(barrier, inc=1, device_id=at_x(d), device_id_type=MESH)
    for d in range(1, NY):
        pl.semaphore_signal(barrier, inc=1, device_id=(dp, lax.rem(y + d, NY)), device_id_type=MESH)
    for d in range(1, NZ):
        pl.semaphore_signal(barrier, inc=1, device_id=at_z(d), device_id_type=MESH)
    pl.semaphore_wait(barrier, 1 + NX - 1 + NY - 1 + NZ - 1)

    def remote(src, dst, sems, slot, peer):
        return pltpu.make_async_remote_copy(
            src_ref=src, dst_ref=dst, send_sem=sems.at[0, slot], recv_sem=sems.at[1, slot],
            device_id=peer, device_id_type=MESH)


    def core_copy(k):
        return remote(wpart.at[(1 - core) * NX + k], core_recv.at[k], core_sem, k, sibling)

    def x_copy(d):
        return remote(x_send.at[lax.rem(x + d, NX)], x_recv.at[d], x_sem, d, at_x(d))

    def z_copy(d):
        return remote(z_send.at[lax.rem(z + d, NZ)], z_recv.at[d], z_sem, d, at_z(d))

    def y_copy(d):
        peer = lax.rem(y + d, NY)
        return remote(y_send.at[peer], y_recv.at[d], y_sem, d, (dp, peer))

    for d in range(1, NX + 1):
        core_copy(lax.rem(x + d, NX)).start()
    for d in range(1, NX):
        k = lax.rem(x + d, NX)
        core_copy(k).wait_recv()
        for t in range(NY):
            x_send[k, t] = (wpart[core * NX + k, t].astype(F32) + core_recv[k, t].astype(F32)).astype(BF16)
        x_copy(d).start()
    core_copy(x).wait_recv()

    for d in range(1, NX):
        x_copy(d).wait_recv()
    for t in range(NY):
        total = wpart[q, t].astype(F32) + core_recv[x, t].astype(F32)
        for d in range(1, NX):
            total = total + x_recv[d, t].astype(F32)
        total = total.astype(BF16)
        for rg in range(3):
            for cg in range(4):
                z_send[rg * 4 + cg, t] = total[16 * rg:16 * rg + 16, 128 * cg:128 * cg + 128]

    def z_start(d, c):
        z_copy(d).start()
        return c

    def z_wait(d, c):
        z_copy(d).wait_recv()
        return c

    lax.fori_loop(1, NZ, z_start, 0)
    lax.fori_loop(1, NZ, z_wait, 0)

    total = z_send[z].astype(F32)
    for d in range(1, NZ):
        total = total + z_recv[d].astype(F32)
    y_send[...] = total

    for d in range(1, NY):
        y_copy(d).start()
    final = y_send[y]
    for d in range(1, NY):
        y_copy(d).wait_recv()
        final = final + y_recv[d]
    final = final / (2 * NX * NZ)

    own = (
        pl.ds(pl.multiple_of(q * 48 + 16 * lax.div(z, 4), 16), 16),
        pl.ds(pl.multiple_of(128 * lax.rem(z, 4), 128), 128),
    )
    comb[own] = final

    def zg_copy(d):
        return remote(comb.at[own], comb.at[own], zg_sem, d, at_z(d))

    def xg_copy(d):
        rows = pl.ds(pl.multiple_of(q * 48, 16), 48)
        return remote(comb.at[rows], comb.at[rows], xg_sem, d, at_x(d))

    rows = pl.ds(pl.multiple_of(core * 192, 16), 192)
    cg_copy = remote(comb.at[rows], comb.at[rows], cg_sem, 0, sibling)

    def zg_start(d, c):
        zg_copy(d).start()
        return c

    def zg_wait(d, c):
        zg_copy(d).wait_recv()
        return c

    lax.fori_loop(1, NZ, zg_start, 0)
    lax.fori_loop(1, NZ, zg_wait, 0)
    for d in range(1, NX):
        xg_copy(d).start()
    for d in range(1, NX):
        xg_copy(d).wait_recv()
    cg_copy.start()
    cg_copy.wait_recv()

    for k in range(8):
        hot_out[0, 32 * k:32 * k + 32, :] = comb[48 * k:48 * k + 32, :]
        cold_out[0, 16 * k:16 * k + 16, :] = comb[48 * k + 32:48 * k + 48, :]

    cg_copy.wait_send()
    for k in range(NX):
        core_copy(k).wait_send()
    for d in range(1, NX):
        x_copy(d).wait_send()
        xg_copy(d).wait_send()
    for d in range(1, NY):
        y_copy(d).wait_send()

    def z_sent(d, c):
        z_copy(d).wait_send()
        zg_copy(d).wait_send()
        return c

    lax.fori_loop(1, NZ, z_sent, 0)


def vmem(*shape, dtype=BF16):
    return pltpu.VMEM(shape, dtype)


def local(
    hot_rows, hot_index, hot_bag, cold_rows, cold_index, cold_bag, hot_proj, cold_proj, cotangent
):
    whole = pl.BlockSpec(memory_space=pltpu.VMEM)
    sem = pltpu.SemaphoreType.DMA
    inter, hot_grads, cold_grads, wpart = pl.pallas_call(
        main_kernel,
        out_shape=(
            jax.ShapeDtypeStruct((SB, 256), F32),
            jax.ShapeDtypeStruct((1, 1, ROWS, WH), F32),
            jax.ShapeDtypeStruct((1, 1, ROWS, WC), F32),
            jax.ShapeDtypeStruct((8, NY, 48, D), BF16),
        ),
        in_specs=[whole] * 9,
        out_specs=(whole,) * 4,
        scratch_shapes=[
            vmem(LOOK, WH), vmem(LOOK, WC),
            vmem(NY, SB, WH), vmem(NY, SB, WC), vmem(NY, SB, WH), vmem(NY, SB, WC),
            vmem(NY, WH, D), vmem(NY, WC, D),
            vmem(ROWS, LOOK), vmem(ROWS, GB), vmem(ROWS, GB),
            vmem(8, 256, 256), vmem(8, 256, 256),
            vmem(2 * NY, SB, D), vmem(2 * NY, SB, D),
            vmem(NY, SB, WH), vmem(NY, SB, WC), vmem(NY, SB, WH), vmem(NY, SB, WC),
            sem((4, NY)), sem((4, NY)), sem((4, 4)), sem((4, 4)), sem((4, NY)),
        ],
        compiler_params=pltpu.CompilerParams(
            collective_id=0, has_side_effects=True, vmem_limit_bytes=VMEM_LIMIT),
    )(hot_rows, hot_index, hot_bag, cold_rows, cold_index, cold_bag, hot_proj, cold_proj, cotangent)
    hot_sum, cold_sum = pl.pallas_call(
        reduce_kernel,
        out_shape=(
            jax.ShapeDtypeStruct((1, WH, D), F32),
            jax.ShapeDtypeStruct((1, WC, D), F32),
        ),
        in_specs=[whole],
        out_specs=(whole,) * 2,
        scratch_shapes=[
            vmem(NX, NY, 48, D), vmem(NX, NY, 48, D), vmem(NX, NY, 48, D),
            vmem(NZ, NY, 16, 128), vmem(NZ, NY, 16, 128),
            vmem(NY, 16, 128, dtype=F32), vmem(NY, 16, 128, dtype=F32), vmem(384, D, dtype=F32),
            sem((2, NX)), sem((2, NX)), sem((2, NZ)), sem((2, NY)), sem((2, NZ)), sem((2, NX)), sem((2, 1)),
        ],
        compiler_params=pltpu.CompilerParams(
            collective_id=1, has_side_effects=True, vmem_limit_bytes=VMEM_LIMIT),
    )(wpart)
    return inter, hot_sum, cold_sum, hot_grads, cold_grads


def solution(mesh):
    return jax.shard_map(
        local,
        mesh=mesh,
        in_specs=(
            P("dp", "table", None, None),
            P("dp", "table", None),
            P("dp", "table", None),
            P("dp", "table", None, None),
            P("dp", "table", None),
            P("dp", "table", None),
            P("table", None, None),
            P("table", None, None),
            P(("dp", "table"), None),
        ),
        out_specs=(
            P(("dp", "table"), None),
            P("table", None, None),
            P("table", None, None),
            P("dp", "table", None, None),
            P("dp", "table", None, None),
        ),
        check_vma=False,
    )
```

time: 472 us -> 155 us (0.33)
  waiting for transfers between devices: 305 us -> 0 us
  Pallas kernels: 0 us -> 142 us
  other arithmetic: 99.2 us -> 0 us
  starting transfers between devices: 22.3 us -> 0 us
  matrix products: 16.6 us -> 0 us
  between operations: 14.1 us -> 0.67 us
    psum x1 -> x0, waiting for transfers between devices: 227 us -> none  [local(): hot_wsum, cold_wsum = lax.psum((hot_wpart, cold_wpart), 'dp')]
    pallas_call x0 -> x2, Pallas kernels: none -> 142 us  [the longest x1 71.4 us: local(): pl.pallas_call(main_kernel, out_shape=(jax.ShapeDtypeStruct((SB, 256), F3...]
    unnamed x11 -> x0, other arithmetic: 94.5 us -> none
    all_to_all x4 -> x0, waiting for transfers between devices: 68.6 us -> none  [the longest x1 25.7 us: local(): lax.all_to_all(grad_feat[:hot_count], 'table', split_axis=0, concat_axis=...]
    all_to_all x4 -> x0, starting transfers between devices: 22 us -> none  [the longest x1 7.61 us: local(): lax.all_to_all(cold_pooled, 'table', split_axis=1, concat_axis=0, tiled=T...]
    dot_general x8 -> x0, matrix products: 16.6 us -> none  [the longest x1 5.61 us: local(): jnp.einsum('tbd,ubd->btu', features, features, preferred_element_type=jnp...]
    all_gather x2 -> x0, waiting for transfers between devices: 7.63 us -> none  [the longest x1 7.62 us: local(): lax.all_gather(hot_proj, 'table', axis=0, tiled=True)]
    unnamed x31 -> x23, local copies, waits for them, and re-layouts: 7.56 us -> 11.4 us
  transfers between devices with their start and end apart: 7 -> 0, of which waited for: 5 -> 0; matrix products, arithmetic and copies ran while one was open for 25% -> 0% of each run, Pallas kernels for 0% -> 0%
where the time goes in v1:
time: 155 us; the launch traced here: 154 us
  Pallas kernels  142 us (92%)
  local copies, waits for them, and re-layouts  11.4 us (7%)
    pallas_call x1, Pallas kernels, local(): pl.pallas_call(main_kernel, out_shape=(jax.ShapeDtypeStruct((SB, 256), F3...  71.4 us
    pallas_call x1, Pallas kernels, local(): pl.pallas_call(reduce_kernel, out_shape=(jax.ShapeDtypeStruct((1, WH, D),...  70.7 us
    unnamed x23, local copies, waits for them, and re-layouts  11.4 us

profile of v1, /device:TPU:1, one launch (start us, length us, event | category | flops | bytes accessed | tf_op | source)
XLA Modules:
  0.0 154.2 jit_solution(13085739120175528016)
XLA Ops:
  0.6 0.0 copy-start
  0.6 1.0 copy-done
  1.7 0.9 copy-done.1
  2.6 0.0 copy-start.2
  2.6 0.9 copy-done.2
  3.6 0.0 copy-start.3
  3.6 0.9 copy-done.3
  4.5 0.0 copy-start.4
  4.5 0.9 copy-done.4
  5.4 0.0 copy-start.5
  5.4 0.7 copy-done.5
  6.1 0.0 copy-start.6
  6.1 0.7 copy-done.6
  6.8 0.0 copy-start.7
  6.8 0.7 copy-done.7
  7.5 0.0 copy-start.8
  7.5 0.7 copy-done.8
  8.2 71.4 %shard_map.128 = (f32[128,256]{1,0:T(8,128)S(1)}, f32[1,1,1024,256]{3,2,1,0:T(8,128)S(1)}, f32[1,1,1024,128]{3,2,1,0:T(8,128)S(1)}, bf16[8,8,48,512]{3,2,1,0:T(8,128)(2,1)S(1)}) custom-call(bf16[1,1,1024,256]{3,2,1,0:T(8,128)(2,1)S(1)} %copy-done, s32[1,1,2048]{2,1,0:T(1,128)S(1)} %copy-done.5, s32[1,1,2048]{2,1,0:T(1,128)S(1)} %copy-done.6, ...), custom_call_target="tpu_custom_call" | custom-call | tf_op jit(solution)/shard_map/pallas_call | solution.py:512
  79.6 70.7 %shard_map.129 = (f32[1,256,512]{2,1,0:T(8,128)S(1)}, f32[1,128,512]{2,1,0:T(8,128)S(1)}) custom-call(bf16[8,8,48,512]{3,2,1,0:T(8,128)(2,1)S(1)} %get-tuple-element.12.wpart), custom_call_target="tpu_custom_call" | custom-call | tf_op jit(solution)/shard_map/pallas_call | solution.py:535
  150.3 0.7 copy.19
  151.0 0.8 copy.20
  151.7 0.7 copy.21
  152.5 1.0 copy.22
  153.4 0.8 copy.23
  (1 shorter events, 0.0 us)
Async XLA Ops:
  0.6 1.0 copy-start
  1.7 0.9 copy-start.1
  2.6 0.9 copy-start.2
  3.6 0.9 copy-start.3
  4.5 0.9 copy-start.4
  5.4 0.7 copy-start.5
  6.1 0.7 copy-start.6
  6.8 0.7 copy-start.7
  7.5 0.7 copy-start.8

commit v2 on v1

v2 whole, which is shorter than its diff:
```python
import math

import jax
import jax.numpy as jnp
from jax import lax
from jax.experimental import pallas as pl
from jax.experimental.pallas import tpu as pltpu
from jax.sharding import PartitionSpec as P

F32 = jnp.float32
BF16 = jnp.bfloat16
MESH = pl.DeviceIdType.MESH
NY = 8
NX = 4
NZ = 12
WH, WC, D = 256, 128, 512
SB = 128
GB = 1024
LOOK = 2048
ROWS = 1024
BAND = 1152
VMEM_LIMIT = 56 * 1024 * 1024
CHUNKS = 4
CW = D // CHUNKS
PICK = 512


def place():
    dp = lax.axis_index("dp")
    y = lax.axis_index("table")
    core = lax.rem(dp, 2)
    x = lax.rem(lax.div(dp, 2), NX)
    z = lax.div(dp, 2 * NX)
    return dp, y, z, x, core


def dot(a, b):
    return jnp.dot(a, b, preferred_element_type=F32)


def dot_nt(a, b):
    return lax.dot_general(a, b, (((1,), (1,)), ((), ())), preferred_element_type=F32)


def dot_tn(a, b):
    return lax.dot_general(a, b, (((0,), (0,)), ((), ())), preferred_element_type=F32)


def iota(shape, dim):
    return lax.broadcasted_iota(jnp.int32, shape, dim)


def split2(v):
    hi = v.astype(BF16)
    return hi, (v - hi.astype(F32)).astype(BF16)


def main_kernel(
    hot_rows_in, hot_index_in, hot_bag_in, cold_rows_in, cold_index_in, cold_bag_in, hot_proj_in, cold_proj_in, cot_in,
    inter, hot_sum, cold_sum, hot_grads, cold_grads,
    hot_rows, hot_index, hot_bag, cold_rows, cold_index, cold_bag, hot_proj, cold_proj, cot,
    hot_picked, cold_picked, hot_send, cold_send, hot_recv, cold_recv,
    hot_w, cold_w, one_index, hot_at, cold_at, m_hi, m_lo, feat, grad,
    hot_bsend, cold_bsend, hot_back, cold_back,
    wpart, core_recv, xs1, xr1, xs2, xr2, z_send, z_recv, y_send, y_recv, comb,
    in_sem, pool_sem, proj_sem, pair_sem, x_sem, core_sem, back_sem,
    wc_sem, wx1_sem, wx2_sem, wz_sem, wy_sem, zg_sem, xg_sem, cg_sem,
):
    dp, y, z, x, core = place()
    q = core * NX + x
    right = lax.rem(x + 1, NX)
    left = lax.rem(x + NX - 1, NX)
    far = lax.rem(x + 2, NX)

    loads = {}
    for n, (name, src, dst) in enumerate((
        ("hot_index", hot_index_in, hot_index), ("hot_rows", hot_rows_in, hot_rows), ("hot_bag", hot_bag_in, hot_bag),
        ("hot_proj", hot_proj_in, hot_proj), ("cold_proj", cold_proj_in, cold_proj),
        ("cold_index", cold_index_in, cold_index), ("cold_rows", cold_rows_in, cold_rows),
        ("cold_bag", cold_bag_in, cold_bag), ("cot", cot_in, cot),
    )):
        loads[name] = pltpu.make_async_copy(src, dst, in_sem.at[n])
        loads[name].start()

    def at_x(other):
        return ((z * NX + other) * 2 + core, y)

    def at_y(d):
        return (dp, lax.rem(y + d, NY))

    def at_z(d):
        return ((lax.rem(z + d, NZ) * NX + x) * 2 + core, y)

    sibling = (dp + 1 - 2 * core, y)

    def remote(src, dst, sems, slot, peer):
        return pltpu.make_async_remote_copy(
            src_ref=src, dst_ref=dst, send_sem=sems.at[(0,) + slot], recv_sem=sems.at[(1,) + slot],
            device_id=peer, device_id_type=MESH)

    barrier = pltpu.get_barrier_semaphore()

    def greet(peer):
        pl.semaphore_signal(barrier, inc=1, device_id=peer, device_id_type=MESH)

    def greet_y(d, c):
        greet(at_y(d))
        return c

    def greet_z(d, c):
        greet(at_z(d))
        return c

    lax.fori_loop(1, NY, greet_y, 0)
    for peer in (at_x(right), at_x(left), at_x(far), sibling):
        greet(peer)
    lax.fori_loop(1, NZ, greet_z, 0)

    def hslice(block):
        return pl.ds(pl.multiple_of(block * 32, 32), 32)

    def cslice(block):
        return pl.ds(pl.multiple_of(block * 16, 16), 16)

    pair = lax.rem(z, 2)

    def columns(n):
        block = lax.rem(2 * pair + n, CHUNKS)
        return pl.ds(pl.multiple_of(block * CW, CW), CW)

    def proj_copies(d, n):
        hot, cold = (hslice(q), columns(n)), (cslice(q), columns(n))
        return (
            remote(hot_proj.at[(0,) + hot], hot_w.at[(y,) + hot], proj_sem, (0, d, n), at_y(d)),
            remote(cold_proj.at[(0,) + cold], cold_w.at[(y,) + cold], proj_sem, (1, d, n), at_y(d)),
        )

    def pair_copies(n):
        hot, cold = hot_w.at[:, hslice(q), columns(n)], cold_w.at[:, cslice(q), columns(n)]
        return (
            remote(hot, hot, pair_sem, (0, n), at_z(1 - 2 * pair + NZ)),
            remote(cold, cold, pair_sem, (1, n), at_z(1 - 2 * pair + NZ)),
        )

    lane = iota((PICK, 128), 1)

    def pick(index, rows, picked):
        def chunk(k, c):
            own = jnp.concatenate([
                jnp.broadcast_to(index[0, :, pl.ds(pl.multiple_of(k * PICK + 128 * i, 128), 128)], (128, 128)).T
                for i in range(PICK // 128)
            ], axis=0)
            hit = jnp.concatenate([(own == lane + 128 * r).astype(F32).astype(BF16) for r in range(8)], axis=1)
            picked[pl.ds(pl.multiple_of(k * PICK, PICK), PICK), :] = dot(hit, rows[0, 0]).astype(BF16)
            return c

        lax.fori_loop(0, LOOK // PICK, chunk, 0, unroll=2)

    def bag_hits(bag, block, samples, width):
        band = pl.ds(pl.multiple_of(block * SB, SB), width)
        ids = iota((samples, width), 0) + block * SB
        return band, (bag[0, :, band] == ids).astype(F32).astype(BF16)

    def pool_copy(which, d):
        send, recv = ((hot_send, hot_recv), (cold_send, cold_recv))[which]
        peer = lax.rem(y + d, NY)
        return pltpu.make_async_remote_copy(
            src_ref=send.at[peer], dst_ref=recv.at[y],
            send_sem=pool_sem.at[2 * which, d], recv_sem=pool_sem.at[2 * which + 1, d],
            device_id=(dp, peer), device_id_type=MESH)

    def pool(which, bag, picked):
        send, recv = ((hot_send, hot_recv), (cold_send, cold_recv))[which]

        def block(d, c):
            peer = lax.rem(y + d, NY)
            band, hits = bag_hits(bag, peer, SB, BAND)
            send[peer] = dot(hits, picked[band, :]).astype(BF16)
            pool_copy(which, d).start()
            return c

        lax.fori_loop(1, NY, block, 0, unroll=True)
        band, hits = bag_hits(bag, y, SB, BAND)
        recv[y] = dot(hits, picked[band, :]).astype(BF16)

    loads["hot_index"].wait()
    loads["hot_rows"].wait()
    pick(hot_index, hot_rows, hot_picked)
    loads["hot_proj"].wait()
    loads["cold_proj"].wait()
    loads["hot_bag"].wait()
    pl.semaphore_wait(barrier, NY - 1 + NZ - 1 + 4)

    for n in range(2):
        def start_proj(d, c):
            for copy in proj_copies(d, n):
                copy.start()
            return c

        lax.fori_loop(1, NY, start_proj, 0)
    for n in range(2):
        hot_w[y, hslice(q), columns(n)] = hot_proj[0, hslice(q), columns(n)]
        cold_w[y, cslice(q), columns(n)] = cold_proj[0, cslice(q), columns(n)]

    def ways(tables, block, n, sems, slot, peer):
        hot = hot_w.at[tables, hslice(block), columns(n)]
        cold = cold_w.at[tables, cslice(block), columns(n)]
        return remote(hot, hot, sems, (0, slot, n), peer), remote(cold, cold, sems, (1, slot, n), peer)

    every, low, high = pl.ds(0, NY), pl.ds(0, NY // 2), pl.ds(NY // 2, NY // 2)
    steps_x = [(
        ways(every, q, n, x_sem, 0, at_x(right)),
        ways(every, q, n, x_sem, 1, at_x(left)),
        ways(low, core * NX + left, n, x_sem, 2, at_x(right)),
        ways(high, core * NX + right, n, x_sem, 3, at_x(left)),
    ) for n in range(CHUNKS)]
    steps_core = [tuple(
        ways(every, core * NX + other, n, core_sem, slot, sibling) for slot, other in enumerate((x, left, right, far))
    ) for n in range(CHUNKS)]

    def start(copies):
        for copy in copies:
            copy.start()

    def arrived(copies):
        for copy in copies:
            copy.wait_recv()

    def first_leg(n):
        def proj_arrived(d, c):
            arrived(proj_copies(d, n))
            return c

        lax.fori_loop(1, NY, proj_arrived, 0)
        start(steps_x[n][0])
        start(steps_x[n][1])
        start(pair_copies(n))
        start(steps_core[n][0])

    def second_leg(n):
        arrived(pair_copies(n))
        start(steps_x[2 + n][0])
        start(steps_x[2 + n][1])
        start(steps_core[2 + n][0])

    def third_leg(n):
        arrived(steps_x[n][0])
        start(steps_x[n][2])
        start(steps_core[n][1])
        arrived(steps_x[n][1])
        start(steps_x[n][3])
        start(steps_core[n][2])

    def fourth_leg(n):
        arrived(steps_x[n][2])
        arrived(steps_x[n][3])
        start(steps_core[n][3])

    pool(0, hot_bag, hot_picked)
    first_leg(0)
    loads["cold_index"].wait()
    loads["cold_rows"].wait()
    pick(cold_index, cold_rows, cold_picked)
    first_leg(1)
    loads["cold_bag"].wait()
    pool(1, cold_bag, cold_picked)
    second_leg(0)
    third_leg(0)
    second_leg(1)

    def onehots(index):
        def onehot(k, c):
            rows = pl.ds(pl.multiple_of(k * 128, 128), 128)
            one_index[rows, :] = (index[0] == iota((128, LOOK), 0) + k * 128).astype(F32).astype(BF16)
            return c

        lax.fori_loop(0, ROWS // 128, onehot, 0)

    def counts(bag, out, first, last):
        def column(j, c):
            width = BAND + SB
            band = pl.ds(pl.multiple_of(2 * j * SB, SB), width)
            ids = iota((2 * SB, width), 0) + 2 * SB * j
            hits = (bag[0, :, band] == ids).astype(F32).astype(BF16)
            out[:, pl.ds(pl.multiple_of(j * 2 * SB, 2 * SB), 2 * SB)] = dot_nt(one_index[:, band], hits).astype(BF16)
            return c

        lax.fori_loop(first, last, column, 0)

    row = iota((256, 256), 0)
    col = iota((256, 256), 1)
    row_hi, row_lo = lax.shift_right_logical(row, 4), lax.bitwise_and(row, 15)
    col_hi, col_lo = lax.shift_right_logical(col, 4), lax.bitwise_and(col, 15)

    def ones(mask):
        return mask.astype(F32).astype(BF16)

    turn = ones((row_hi == col_lo) & (row_lo == col_hi))
    widen = ones(row_lo == col_hi)
    narrow = ones(row_hi == col_lo)
    same_hi = row_hi == col_hi
    same_lo = row_lo == col_lo

    def spread_cot(g, c):
        rows = pl.ds(pl.multiple_of(g * 16, 16), 16)
        part = cot[rows, :]
        hi, lo = split2(part)
        sym = part + (dot(hi, turn) + dot(lo, turn))
        tall = jnp.where(same_hi, jnp.concatenate([sym] * 16, axis=0), 0.0)
        hi, lo = split2(tall)
        m_hi[g] = jnp.where(same_lo, dot(hi, widen), 0.0).astype(BF16)
        m_lo[g] = jnp.where(same_lo, dot(lo, widen), 0.0).astype(BF16)
        return c

    loads["cot"].wait()
    lax.fori_loop(0, SB // 16, spread_cot, 0, unroll=4)
    third_leg(1)
    onehots(hot_index)
    third_leg(2)
    counts(hot_bag, hot_at, 0, 2)
    third_leg(3)
    fourth_leg(0)
    fourth_leg(1)
    counts(hot_bag, hot_at, 2, 4)
    fourth_leg(2)
    fourth_leg(3)
    onehots(cold_index)
    for n in range(CHUNKS):
        for copies in steps_core[n]:
            arrived(copies)

    def hot_features(d, c):
        t = lax.rem(y - d + NY, NY)
        feat[t] = dot(hot_recv[t], hot_w[t]).astype(BF16)
        return c

    def cold_features(d, c):
        t = lax.rem(y - d + NY, NY)
        feat[NY + t] = dot(cold_recv[t], cold_w[t]).astype(BF16)
        return c

    def pool_arrived(which):
        def one(d, c):
            pool_copy(which, d).wait_recv()
            return c

        lax.fori_loop(1, NY, one, 0)

    pool_arrived(0)
    lax.fori_loop(0, NY, hot_features, 0, unroll=True)
    counts(cold_bag, cold_at, 0, 2)
    pool_arrived(1)
    lax.fori_loop(0, NY, cold_features, 0, unroll=True)

    root_scale = 1.0 / math.sqrt(D)

    def sixteen(g, c):
        rows = pl.ds(pl.multiple_of(g * 16, 16), 16)
        block = feat[:, rows, :].reshape(256, D)
        gram = jnp.where(same_lo, dot_nt(block, block) * root_scale, 0.0)
        hi, lo = split2(gram)
        wide = jnp.where(same_hi, dot(hi, narrow) + dot(lo, narrow), 0.0)
        inter[rows, :] = jnp.sum(wide.reshape(16, 16, 256), axis=0)
        slope = (dot(m_hi[g], block) + dot(m_lo[g], block)) * root_scale
        grad[:, rows, :] = slope.astype(BF16).reshape(16, 16, D)
        return c

    lax.fori_loop(0, SB // 16, sixteen, 0, unroll=4)


    def back_copy(which, d):
        send, recv = ((hot_bsend, hot_back), (cold_bsend, cold_back))[which]
        peer = lax.rem(y + d, NY)
        return pltpu.make_async_remote_copy(
            src_ref=send.at[peer], dst_ref=recv.at[y],
            send_sem=back_sem.at[2 * which, d], recv_sem=back_sem.at[2 * which + 1, d],
            device_id=(dp, peer), device_id_type=MESH)

    def hot_return(d, c):
        peer = lax.rem(y + d, NY)
        hot_bsend[peer] = dot_nt(grad[peer], hot_w[peer]).astype(BF16)
        back_copy(0, d).start()
        return c

    def cold_return(d, c):
        peer = lax.rem(y + d, NY)
        cold_bsend[peer] = dot_nt(grad[NY + peer], cold_w[peer]).astype(BF16)
        back_copy(1, d).start()
        return c

    def weight_part(t, c):
        wpart[:, t, 0:32, :] = dot_tn(hot_recv[t], grad[t]).astype(BF16).reshape(8, 32, D)
        wpart[:, t, 32:48, :] = dot_tn(cold_recv[t], grad[NY + t]).astype(BF16).reshape(8, 16, D)
        return c

    def wc_copy(k):
        pair = pl.ds(2 * k, 2)
        return remote(wpart.at[pl.ds((1 - core) * NX, NX), pair], core_recv.at[:, pair], wc_sem, (k,), sibling)

    def wx1_copy(k, way):
        return remote(xs1.at[k, way], xr1.at[k, way], wx1_sem, (k, way), at_x((right, left)[way]))

    def wx2_copy(k, way):
        return remote(xs2.at[k, way], xr2.at[k, way], wx2_sem, (k, way), at_x((right, left)[way]))

    def wz_copy(k, d):
        group = pl.ds(2 * k, 2)
        return remote(z_send.at[lax.rem(z + d, NZ), group], z_recv.at[d, group], wz_sem, (k, d), at_z(d))

    def wy_copy(d):
        return remote(y_send.at[lax.rem(y + d, NY)], y_recv.at[d], wy_sem, (d,), at_y(d))

    def both(other, t):
        return wpart[core * NX + other, t].astype(F32) + core_recv[other, t].astype(F32)

    def part(k):
        weight_part(2 * k, 0)
        weight_part(2 * k + 1, 0)
        wc_copy(k).start()

    def stage_core(k):
        wc_copy(k).wait_recv()
        xs1[k, 0, 0] = both(far, 2 * k).astype(BF16)
        xs1[k, 0, 1] = both(right, 2 * k + 1).astype(BF16)
        wx1_copy(k, 0).start()
        xs1[k, 1, 0] = both(far, 2 * k + 1).astype(BF16)
        xs1[k, 1, 1] = both(left, 2 * k).astype(BF16)
        wx1_copy(k, 1).start()

    def stage_x(k):
        wx1_copy(k, 0).wait_recv()
        xs2[k, 0] = (both(right, 2 * k) + xr1[k, 0, 0].astype(F32)).astype(BF16)
        wx2_copy(k, 0).start()
        wx1_copy(k, 1).wait_recv()
        xs2[k, 1] = (both(left, 2 * k + 1) + xr1[k, 1, 0].astype(F32)).astype(BF16)
        wx2_copy(k, 1).start()

    def stage_sum(k):
        wx2_copy(k, 0).wait_recv()
        wx2_copy(k, 1).wait_recv()
        for t, one, two in ((2 * k, xr2[k, 0], xr1[k, 1, 1]), (2 * k + 1, xr1[k, 0, 1], xr2[k, 1])):
            total = (both(x, t) + one.astype(F32) + two.astype(F32)).astype(BF16)
            for rg in range(3):
                for cg in range(4):
                    z_send[rg * 4 + cg, t] = total[16 * rg:16 * rg + 16, 128 * cg:128 * cg + 128]

    def stage_z(k):
        def one(d, c):
            wz_copy(k, d).start()
            return c

        lax.fori_loop(1, NZ, one, 0)

    def z_total(k):
        def one(d, c):
            wz_copy(k, d).wait_recv()
            return c

        lax.fori_loop(1, NZ, one, 0)
        group = slice(2 * k, 2 * k + 2)
        total = z_send[z, group].astype(F32)
        for d in range(1, NZ):
            total = total + z_recv[d, group].astype(F32)
        y_send[group] = total

    def back_arrived(which):
        def one(d, c):
            back_copy(which, d).wait_recv()
            return c

        lax.fori_loop(1, NY, one, 0)

    def spread(at, back, out, width):
        out[0, 0] = dot(at[...], back[...].reshape(GB, width))

    part(0)
    part(1)
    stage_core(0)
    part(2)
    stage_core(1)
    part(3)
    lax.fori_loop(1, NY, hot_return, 0, unroll=True)
    stage_core(2)
    stage_x(0)
    lax.fori_loop(1, NY, cold_return, 0, unroll=True)
    stage_core(3)
    stage_x(1)
    stage_sum(0)
    stage_z(0)
    stage_x(2)
    stage_sum(1)
    stage_z(1)
    hot_back[y] = dot_nt(grad[y], hot_w[y]).astype(BF16)
    cold_back[y] = dot_nt(grad[NY + y], cold_w[y]).astype(BF16)
    stage_x(3)
    stage_sum(2)
    stage_z(2)
    stage_sum(3)
    stage_z(3)
    counts(cold_bag, cold_at, 2, 4)
    z_total(0)
    z_total(1)
    z_total(2)
    z_total(3)
    for d in range(1, NY):
        wy_copy(d).start()
    back_arrived(0)
    spread(hot_at, hot_back, hot_grads, WH)
    final = y_send[y]
    for d in range(1, NY):
        wy_copy(d).wait_recv()
        final = final + y_recv[d]
    final = final / (2 * NX * NZ)

    own = (
        pl.ds(pl.multiple_of(q * 48 + 16 * lax.div(z, 4), 16), 16),
        pl.ds(pl.multiple_of(128 * lax.rem(z, 4), 128), 128),
    )
    comb[own] = final.astype(BF16)

    def zg_copy(d):
        return remote(comb.at[own], comb.at[own], zg_sem, (d,), at_z(d))

    def xg_copy(d):
        rows = pl.ds(pl.multiple_of(q * 48, 16), 48)
        return remote(comb.at[rows], comb.at[rows], xg_sem, (d,), at_x(lax.rem(x + d, NX)))

    rows = pl.ds(pl.multiple_of(core * 192, 16), 192)
    cg_copy = remote(comb.at[rows], comb.at[rows], cg_sem, (0,), sibling)

    def zg_start(d, c):
        zg_copy(d).start()
        return c

    def zg_wait(d, c):
        zg_copy(d).wait_recv()
        return c

    lax.fori_loop(1, NZ, zg_start, 0)
    back_arrived(1)
    spread(cold_at, cold_back, cold_grads, WC)
    lax.fori_loop(1, NZ, zg_wait, 0)
    for d in range(1, NX):
        xg_copy(d).start()
    for d in range(1, NX):
        xg_copy(d).wait_recv()
    cg_copy.start()
    cg_copy.wait_recv()

    for k in range(8):
        hot_sum[0, 32 * k:32 * k + 32, :] = comb[48 * k:48 * k + 32, :].astype(F32)
        cold_sum[0, 16 * k:16 * k + 16, :] = comb[48 * k + 32:48 * k + 48, :].astype(F32)

    def sent_y(d, c):
        for n in range(2):
            for copy in proj_copies(d, n):
                copy.wait_send()
        for which in range(2):
            pool_copy(which, d).wait_send()
            back_copy(which, d).wait_send()
        wy_copy(d).wait_send()
        return c

    def sent_z(d, c):
        for k in range(4):
            wz_copy(k, d).wait_send()
        zg_copy(d).wait_send()
        return c

    lax.fori_loop(1, NY, sent_y, 0)
    lax.fori_loop(1, NZ, sent_z, 0)
    for n in range(CHUNKS):
        for copies in steps_x[n] + steps_core[n]:
            for copy in copies:
                copy.wait_send()
    for n in range(2):
        for copy in pair_copies(n):
            copy.wait_send()
    for k in range(4):
        wc_copy(k).wait_send()
        for way in range(2):
            wx1_copy(k, way).wait_send()
            wx2_copy(k, way).wait_send()
    for d in range(1, NX):
        xg_copy(d).wait_send()
    cg_copy.wait_send()


def store_kernel(*refs):
    sources, targets, sems = refs[:5], refs[5:10], refs[10]
    copies = [pltpu.make_async_copy(sources[n], targets[n], sems.at[n]) for n in range(5)]
    for copy in copies:
        copy.start()
    for copy in copies:
        copy.wait()


def vmem(*shape, dtype=BF16):
    return pltpu.VMEM(shape, dtype)


def local(
    hot_rows, hot_index, hot_bag, cold_rows, cold_index, cold_bag, hot_proj, cold_proj, cotangent
):
    whole = pl.BlockSpec(memory_space=pltpu.VMEM)
    outside = pl.BlockSpec(memory_space=pl.ANY)
    sem = pltpu.SemaphoreType.DMA
    outs = (
        jax.ShapeDtypeStruct((SB, 256), F32),
        jax.ShapeDtypeStruct((1, WH, D), F32),
        jax.ShapeDtypeStruct((1, WC, D), F32),
        jax.ShapeDtypeStruct((1, 1, ROWS, WH), F32),
        jax.ShapeDtypeStruct((1, 1, ROWS, WC), F32),
    )
    ids = vmem(1, 1, LOOK, dtype=jnp.int32)
    args = (hot_rows, hot_index, hot_bag, cold_rows, cold_index, cold_bag, hot_proj, cold_proj, cotangent)
    results = pl.pallas_call(
        main_kernel,
        out_shape=outs,
        in_specs=[outside] * 9,
        out_specs=(whole,) * 5,
        scratch_shapes=[
            vmem(1, 1, ROWS, WH), ids, ids, vmem(1, 1, ROWS, WC), ids, ids,
            vmem(1, WH, D), vmem(1, WC, D), vmem(SB, 256, dtype=F32),
            vmem(LOOK, WH), vmem(LOOK, WC),
            vmem(NY, SB, WH), vmem(NY, SB, WC), vmem(NY, SB, WH), vmem(NY, SB, WC),
            vmem(NY, WH, D), vmem(NY, WC, D),
            vmem(ROWS, LOOK), vmem(ROWS, GB), vmem(ROWS, GB),
            vmem(8, 256, 256), vmem(8, 256, 256),
            vmem(2 * NY, SB, D), vmem(2 * NY, SB, D),
            vmem(NY, SB, WH), vmem(NY, SB, WC), vmem(NY, SB, WH), vmem(NY, SB, WC),
            vmem(8, NY, 48, D), vmem(NX, NY, 48, D),
            vmem(4, 2, 2, 48, D), vmem(4, 2, 2, 48, D), vmem(4, 2, 48, D), vmem(4, 2, 48, D),
            vmem(NZ, NY, 16, 128), vmem(NZ, NY, 16, 128),
            vmem(NY, 16, 128, dtype=F32), vmem(NY, 16, 128, dtype=F32), vmem(384, D),
            sem((9,)), sem((4, NY)), sem((2, 2, NY, 2)), sem((2, 2, 2)), sem((2, 2, 4, CHUNKS)), sem((2, 2, 4, CHUNKS)), sem((4, NY)),
            sem((2, 4)), sem((2, 4, 2)), sem((2, 4, 2)), sem((2, 4, NZ)), sem((2, NY)), sem((2, NZ)), sem((2, NX)), sem((2, 1)),
        ],
        compiler_params=pltpu.CompilerParams(
            collective_id=0, has_side_effects=True, vmem_limit_bytes=VMEM_LIMIT),
    )(*args)
    return tuple(pl.pallas_call(
        store_kernel,
        out_shape=outs,
        in_specs=[whole] * 5,
        out_specs=(outside,) * 5,
        scratch_shapes=[sem((5,))],
    )(*results))


def solution(mesh):
    return jax.shard_map(
        local,
        mesh=mesh,
        in_specs=(
            P("dp", "table", None, None),
            P("dp", "table", None),
            P("dp", "table", None),
            P("dp", "table", None, None),
            P("dp", "table", None),
            P("dp", "table", None),
            P("table", None, None),
            P("table", None, None),
            P(("dp", "table"), None),
        ),
        out_specs=(
            P(("dp", "table"), None),
            P("table", None, None),
            P("table", None, None),
            P("dp", "table", None, None),
            P("dp", "table", None, None),
        ),
        check_vma=False,
    )
```

time: 155 us -> 104 us (0.67)
  Pallas kernels: 142 us -> 103 us
  local copies, waits for them, and re-layouts: 11.4 us -> 0 us
    pallas_call x2, Pallas kernels: 142 us -> 103 us  [the longest x1 99.9 us: local(): pl.pallas_call(main_kernel, out_shape=outs, in_specs=[outside] * 9, out_s...]
    unnamed x23 -> x0, local copies, waits for them, and re-layouts: 11.4 us -> none
where the time goes in v2:
time: 104 us
  Pallas kernels  103 us (99%)
    pallas_call x1, Pallas kernels, local(): pl.pallas_call(main_kernel, out_shape=outs, in_specs=[outside] * 9, out_s...  99.9 us
    pallas_call x1, Pallas kernels, local(): pl.pallas_call(store_kernel, out_shape=outs, in_specs=[whole] * 5, out_sp...  3.12 us

profile of v2, /device:TPU:1, one launch (start us, length us, event | category | flops | bytes accessed | tf_op | source)
XLA Modules:
  0.0 103.9 jit_solution(11836919390929383049)
XLA Ops:
  0.6 99.9 %shard_map.128 = (f32[128,256]{1,0:T(8,128)}, f32[1,256,512]{2,1,0:T(8,128)}, f32[1,128,512]{2,1,0:T(8,128)}, f32[1,1,1024,256]{3,2,1,0:T(8,128)}, f32[1,1,1024,128]{3,2,1,0:T(8,128)}) custom-call(bf16[1,1,1024,256]{3,2,1,0:T(8,128)(2,1)} %hot_rows_in.1, s32[1,1,2048]{2,1,0:T(1,128)} %hot_index_in.1, s32[1,1,2048]{2,1,0:T(1,128)} %hot_bag_in.1, ...), custom_call_target="tpu_custom_call" | custom-call | tf_op jit(solution)/shard_map/pallas_call | solution.py:617
  100.6 3.1 %shard_map.129 = (f32[128,256]{1,0:T(8,128)}, f32[1,256,512]{2,1,0:T(8,128)}, f32[1,128,512]{2,1,0:T(8,128)}, f32[1,1,1024,256]{3,2,1,0:T(8,128)}, f32[1,1,1024,128]{3,2,1,0:T(8,128)}) custom-call(f32[128,256]{1,0:T(8,128)} %get-tuple-element.10.refs_0_, f32[1,256,512]{2,1,0:T(8,128)} %get-tuple-element.11.refs_1_, ...), custom_call_target="tpu_custom_call" | custom-call | tf_op jit(solution)/shard_map/pallas_call | solution.py:642

commit v3 on v2

--- a/solution.py
+++ b/solution.py
@@ -60,7 +60,7 @@
     inter, hot_sum, cold_sum, hot_grads, cold_grads,
     hot_rows, hot_index, hot_bag, cold_rows, cold_index, cold_bag, hot_proj, cold_proj, cot,
     hot_picked, cold_picked, hot_send, cold_send, hot_recv, cold_recv,
-    hot_w, cold_w, one_index, hot_at, cold_at, m_hi, m_lo, feat, grad,
+    proj_w, one_index, hot_at, cold_at, m_hi, m_lo, feat, grad,
     hot_bsend, cold_bsend, hot_back, cold_back,
     wpart, core_recv, xs1, xr1, xs2, xr2, z_send, z_recv, y_send, y_recv, comb,
     in_sem, pool_sem, proj_sem, pair_sem, x_sem, core_sem, back_sem,
@@ -116,31 +116,26 @@
         greet(peer)
     lax.fori_loop(1, NZ, greet_z, 0)
 
-    def hslice(block):
-        return pl.ds(pl.multiple_of(block * 32, 32), 32)
-
-    def cslice(block):
-        return pl.ds(pl.multiple_of(block * 16, 16), 16)
-
     pair = lax.rem(z, 2)
 
+    pair = lax.rem(z, 2)
+
     def columns(n):
-        block = lax.rem(2 * pair + n, CHUNKS)
-        return pl.ds(pl.multiple_of(block * CW, CW), CW)
-
-    def proj_copies(d, n):
-        hot, cold = (hslice(q), columns(n)), (cslice(q), columns(n))
-        return (
-            remote(hot_proj.at[(0,) + hot], hot_w.at[(y,) + hot], proj_sem, (0, d, n), at_y(d)),
-            remote(cold_proj.at[(0,) + cold], cold_w.at[(y,) + cold], proj_sem, (1, d, n), at_y(d)),
-        )
-
-    def pair_copies(n):
-        hot, cold = hot_w.at[:, hslice(q), columns(n)], cold_w.at[:, cslice(q), columns(n)]
-        return (
-            remote(hot, hot, pair_sem, (0, n), at_z(1 - 2 * pair + NZ)),
-            remote(cold, cold, pair_sem, (1, n), at_z(1 - 2 * pair + NZ)),
-        )
+        return lax.rem(2 * pair + n, CHUNKS)
+
+    def proj_copy(d, n):
+        mine = proj_w.at[columns(n), q, y]
+        return remote(mine, mine, proj_sem, (d, n), at_y(d))
+
+    def pair_copy(n):
+        mine = proj_w.at[columns(n), q]
+        return remote(mine, mine, pair_sem, (n,), at_z(1 - 2 * pair + NZ))
+
+    def hot_weights(t):
+        return jnp.concatenate([proj_w[n, :, t, 0:32, :].reshape(WH, CW) for n in range(CHUNKS)], axis=1)
+
+    def cold_weights(t):
+        return jnp.concatenate([proj_w[n, :, t, 32:48, :].reshape(WC, CW) for n in range(CHUNKS)], axis=1)
 
     lane = iota((PICK, 128), 1)
 
@@ -192,69 +187,60 @@
     pl.semaphore_wait(barrier, NY - 1 + NZ - 1 + 4)
 
     for n in range(2):
+        cols = pl.ds(pl.multiple_of(columns(n) * CW, CW), CW)
+        proj_w[columns(n), q, y, 0:32, :] = hot_proj[0, pl.ds(pl.multiple_of(q * 32, 32), 32), cols]
+        proj_w[columns(n), q, y, 32:48, :] = cold_proj[0, pl.ds(pl.multiple_of(q * 16, 16), 16), cols]
+
         def start_proj(d, c):
-            for copy in proj_copies(d, n):
-                copy.start()
+            proj_copy(d, n).start()
             return c
 
         lax.fori_loop(1, NY, start_proj, 0)
-    for n in range(2):
-        hot_w[y, hslice(q), columns(n)] = hot_proj[0, hslice(q), columns(n)]
-        cold_w[y, cslice(q), columns(n)] = cold_proj[0, cslice(q), columns(n)]
-
-    def ways(tables, block, n, sems, slot, peer):
-        hot = hot_w.at[tables, hslice(block), columns(n)]
-        cold = cold_w.at[tables, cslice(block), columns(n)]
-        return remote(hot, hot, sems, (0, slot, n), peer), remote(cold, cold, sems, (1, slot, n), peer)
+
+    def way(tables, block, n, sems, slot, peer):
+        part = proj_w.at[columns(n), block, tables]
+        return remote(part, part, sems, (slot, n), peer)
 
     every, low, high = pl.ds(0, NY), pl.ds(0, NY // 2), pl.ds(NY // 2, NY // 2)
     steps_x = [(
-        ways(every, q, n, x_sem, 0, at_x(right)),
-        ways(every, q, n, x_sem, 1, at_x(left)),
-        ways(low, core * NX + left, n, x_sem, 2, at_x(right)),
-        ways(high, core * NX + right, n, x_sem, 3, at_x(left)),
+        way(every, q, n, x_sem, 0, at_x(right)),
+        way(every, q, n, x_sem, 1, at_x(left)),
+        way(low, core * NX + left, n, x_sem, 2, at_x(right)),
+        way(high, core * NX + right, n, x_sem, 3, at_x(left)),
     ) for n in range(CHUNKS)]
     steps_core = [tuple(
-        ways(every, core * NX + other, n, core_sem, slot, sibling) for slot, other in enumerate((x, left, right, far))
+        way(every, core * NX + other, n, core_sem, slot, sibling) for slot, other in enumerate((x, left, right, far))
     ) for n in range(CHUNKS)]
-
-    def start(copies):
-        for copy in copies:
-            copy.start()
-
-    def arrived(copies):
-        for copy in copies:
-            copy.wait_recv()
 
     def first_leg(n):
         def proj_arrived(d, c):
-            arrived(proj_copies(d, n))
+            proj_copy(d, n).wait_recv()
             return c
 
         lax.fori_loop(1, NY, proj_arrived, 0)
-        start(steps_x[n][0])
-        start(steps_x[n][1])
-        start(pair_copies(n))
-        start(steps_core[n][0])
+        steps_x[n][0].start()
+        steps_x[n][1].start()
+        pair_copy(n).start()
+        steps_core[n][0].start()
 
     def second_leg(n):
-        arrived(pair_copies(n))
-        start(steps_x[2 + n][0])
-        start(steps_x[2 + n][1])
-        start(steps_core[2 + n][0])
+        pair_copy(n).wait_recv()
+        steps_x[2 + n][0].start()
+        steps_x[2 + n][1].start()
+        steps_core[2 + n][0].start()
 
     def third_leg(n):
-        arrived(steps_x[n][0])
-        start(steps_x[n][2])
-        start(steps_core[n][1])
-        arrived(steps_x[n][1])
-        start(steps_x[n][3])
-        start(steps_core[n][2])
+        steps_x[n][0].wait_recv()
+        steps_x[n][2].start()
+        steps_core[n][1].start()
+        steps_x[n][1].wait_recv()
+        steps_x[n][3].start()
+        steps_core[n][2].start()
 
     def fourth_leg(n):
-        arrived(steps_x[n][2])
-        arrived(steps_x[n][3])
-        start(steps_core[n][3])
+        steps_x[n][2].wait_recv()
+        steps_x[n][3].wait_recv()
+        steps_core[n][3].start()
 
     pool(0, hot_bag, hot_picked)
     first_leg(0)
@@ -326,17 +312,17 @@
     fourth_leg(3)
     onehots(cold_index)
     for n in range(CHUNKS):
-        for copies in steps_core[n]:
-            arrived(copies)
+        for copy in steps_core[n]:
+            copy.wait_recv()
 
     def hot_features(d, c):
         t = lax.rem(y - d + NY, NY)
-        feat[t] = dot(hot_recv[t], hot_w[t]).astype(BF16)
+        feat[t] = dot(hot_recv[t], hot_weights(t)).astype(BF16)
         return c
 
     def cold_features(d, c):
         t = lax.rem(y - d + NY, NY)
-        feat[NY + t] = dot(cold_recv[t], cold_w[t]).astype(BF16)
+        feat[NY + t] = dot(cold_recv[t], cold_weights(t)).astype(BF16)
         return c
 
     def pool_arrived(which):
@@ -378,13 +364,13 @@
 
     def hot_return(d, c):
         peer = lax.rem(y + d, NY)
-        hot_bsend[peer] = dot_nt(grad[peer], hot_w[peer]).astype(BF16)
+        hot_bsend[peer] = dot_nt(grad[peer], hot_weights(peer)).astype(BF16)
         back_copy(0, d).start()
         return c
 
     def cold_return(d, c):
         peer = lax.rem(y + d, NY)
-        cold_bsend[peer] = dot_nt(grad[NY + peer], cold_w[peer]).astype(BF16)
+        cold_bsend[peer] = dot_nt(grad[NY + peer], cold_weights(peer)).astype(BF16)
         back_copy(1, d).start()
         return c
 
@@ -490,14 +476,33 @@
     stage_x(2)
     stage_sum(1)
     stage_z(1)
-    hot_back[y] = dot_nt(grad[y], hot_w[y]).astype(BF16)
-    cold_back[y] = dot_nt(grad[NY + y], cold_w[y]).astype(BF16)
+    hot_back[y] = dot_nt(grad[y], hot_weights(y)).astype(BF16)
+    cold_back[y] = dot_nt(grad[NY + y], cold_weights(y)).astype(BF16)
     stage_x(3)
     stage_sum(2)
     stage_z(2)
     stage_sum(3)
     stage_z(3)
     counts(cold_bag, cold_at, 2, 4)
+
+    def sent_forward(d, c):
+        for n in range(2):
+            proj_copy(d, n).wait_send()
+            pool_copy(n, d).wait_send()
+        return c
+
+    lax.fori_loop(1, NY, sent_forward, 0)
+    for n in range(CHUNKS):
+        for copy in steps_x[n] + steps_core[n]:
+            copy.wait_send()
+    for n in range(2):
+        pair_copy(n).wait_send()
+    for k in range(4):
+        wc_copy(k).wait_send()
+        for way in range(2):
+            wx1_copy(k, way).wait_send()
+            wx2_copy(k, way).wait_send()
+
     z_total(0)
     z_total(1)
     z_total(2)
@@ -512,20 +517,16 @@
         final = final + y_recv[d]
     final = final / (2 * NX * NZ)
 
-    own = (
-        pl.ds(pl.multiple_of(q * 48 + 16 * lax.div(z, 4), 16), 16),
-        pl.ds(pl.multiple_of(128 * lax.rem(z, 4), 128), 128),
-    )
-    comb[own] = final.astype(BF16)
+    own = comb.at[q, z]
+    own[...] = final.astype(BF16)
 
     def zg_copy(d):
-        return remote(comb.at[own], comb.at[own], zg_sem, (d,), at_z(d))
+        return remote(own, own, zg_sem, (d,), at_z(d))
 
     def xg_copy(d):
-        rows = pl.ds(pl.multiple_of(q * 48, 16), 48)
-        return remote(comb.at[rows], comb.at[rows], xg_sem, (d,), at_x(lax.rem(x + d, NX)))
-
-    rows = pl.ds(pl.multiple_of(core * 192, 16), 192)
+        return remote(comb.at[q], comb.at[q], xg_sem, (d,), at_x(lax.rem(x + d, NX)))
+
+    rows = pl.ds(core * NX, NX)
     cg_copy = remote(comb.at[rows], comb.at[rows], cg_sem, (0,), sibling)
 
     def zg_start(d, c):
@@ -539,48 +540,40 @@
     lax.fori_loop(1, NZ, zg_start, 0)
     back_arrived(1)
     spread(cold_at, cold_back, cold_grads, WC)
+
+    def sent_y(d, c):
+        back_copy(0, d).wait_send()
+        back_copy(1, d).wait_send()
+        wy_copy(d).wait_send()
+        return c
+
+    def sent_z(d, c):
+        for k in range(4):
+            wz_copy(k, d).wait_send()
+        return c
+
+    def sent_zg(d, c):
+        zg_copy(d).wait_send()
+        return c
+
+    lax.fori_loop(1, NY, sent_y, 0)
+    lax.fori_loop(1, NZ, sent_z, 0)
     lax.fori_loop(1, NZ, zg_wait, 0)
     for d in range(1, NX):
         xg_copy(d).start()
+    lax.fori_loop(1, NZ, sent_zg, 0)
     for d in range(1, NX):
         xg_copy(d).wait_recv()
     cg_copy.start()
     cg_copy.wait_recv()
 
     for k in range(8):
-        hot_sum[0, 32 * k:32 * k + 32, :] = comb[48 * k:48 * k + 32, :].astype(F32)
-        cold_sum[0, 16 * k:16 * k + 16, :] = comb[48 * k + 32:48 * k + 48, :].astype(F32)
-
-    def sent_y(d, c):
-        for n in range(2):
-            for copy in proj_copies(d, n):
-                copy.wait_send()
-        for which in range(2):
-            pool_copy(which, d).wait_send()
-            back_copy(which, d).wait_send()
-        wy_copy(d).wait_send()
-        return c
-
-    def sent_z(d, c):
-        for k in range(4):
-            wz_copy(k, d).wait_send()
-        zg_copy(d).wait_send()
-        return c
-
-    lax.fori_loop(1, NY, sent_y, 0)
-    lax.fori_loop(1, NZ, sent_z, 0)
-    for n in range(CHUNKS):
-        for copies in steps_x[n] + steps_core[n]:
-            for copy in copies:
-                copy.wait_send()
-    for n in range(2):
-        for copy in pair_copies(n):
-            copy.wait_send()
-    for k in range(4):
-        wc_copy(k).wait_send()
-        for way in range(2):
-            wx1_copy(k, way).wait_send()
-            wx2_copy(k, way).wait_send()
+        for cg in range(4):
+            cols = slice(128 * cg, 128 * cg + 128)
+            hot_sum[0, 32 * k:32 * k + 16, cols] = comb[k, cg].astype(F32)
+            hot_sum[0, 32 * k + 16:32 * k + 32, cols] = comb[k, 4 + cg].astype(F32)
+            cold_sum[0, 16 * k:16 * k + 16, cols] = comb[k, 8 + cg].astype(F32)
+
     for d in range(1, NX):
         xg_copy(d).wait_send()
     cg_copy.wait_send()
@@ -624,7 +617,7 @@
             vmem(1, WH, D), vmem(1, WC, D), vmem(SB, 256, dtype=F32),
             vmem(LOOK, WH), vmem(LOOK, WC),
             vmem(NY, SB, WH), vmem(NY, SB, WC), vmem(NY, SB, WH), vmem(NY, SB, WC),
-            vmem(NY, WH, D), vmem(NY, WC, D),
+            vmem(CHUNKS, 8, NY, 48, CW),
             vmem(ROWS, LOOK), vmem(ROWS, GB), vmem(ROWS, GB),
             vmem(8, 256, 256), vmem(8, 256, 256),
             vmem(2 * NY, SB, D), vmem(2 * NY, SB, D),
@@ -632,8 +625,8 @@
             vmem(8, NY, 48, D), vmem(NX, NY, 48, D),
             vmem(4, 2, 2, 48, D), vmem(4, 2, 2, 48, D), vmem(4, 2, 48, D), vmem(4, 2, 48, D),
             vmem(NZ, NY, 16, 128), vmem(NZ, NY, 16, 128),
-            vmem(NY, 16, 128, dtype=F32), vmem(NY, 16, 128, dtype=F32), vmem(384, D),
-            sem((9,)), sem((4, NY)), sem((2, 2, NY, 2)), sem((2, 2, 2)), sem((2, 2, 4, CHUNKS)), sem((2, 2, 4, CHUNKS)), sem((4, NY)),
+            vmem(NY, 16, 128, dtype=F32), vmem(NY, 16, 128, dtype=F32), vmem(8, NZ, 16, 128),
+            sem((9,)), sem((4, NY)), sem((2, NY, 2)), sem((2, 2)), sem((2, 4, CHUNKS)), sem((2, 4, CHUNKS)), sem((4, NY)),
             sem((2, 4)), sem((2, 4, 2)), sem((2, 4, 2)), sem((2, 4, NZ)), sem((2, NY)), sem((2, NZ)), sem((2, NX)), sem((2, 1)),
         ],
         compiler_params=pltpu.CompilerParams(

time: 104 us -> 103 us (level)
    pallas_call x1, Pallas kernels: 99.9 us -> 98.6 us  [local(): pl.pallas_call(main_kernel, out_shape=outs, in_specs=[outside] * 9, out_s...]
where the time goes in v3:
time: 103 us
  Pallas kernels  102 us (99%)
    pallas_call x1, Pallas kernels, local(): pl.pallas_call(main_kernel, out_shape=outs, in_specs=[outside] * 9, out_s...  98.6 us
    pallas_call x1, Pallas kernels, local(): pl.pallas_call(store_kernel, out_shape=outs, in_specs=[whole] * 5, out_sp...  3.12 us

profile of v3, /device:TPU:1, one launch (start us, length us, event | category | flops | bytes accessed | tf_op | source)
XLA Modules:
  0.0 102.5 jit_solution(12827799554177985064)
XLA Ops:
  0.6 98.6 %shard_map.128 = (f32[128,256]{1,0:T(8,128)}, f32[1,256,512]{2,1,0:T(8,128)}, f32[1,128,512]{2,1,0:T(8,128)}, f32[1,1,1024,256]{3,2,1,0:T(8,128)}, f32[1,1,1024,128]{3,2,1,0:T(8,128)}) custom-call(bf16[1,1,1024,256]{3,2,1,0:T(8,128)(2,1)} %hot_rows_in.1, s32[1,1,2048]{2,1,0:T(1,128)} %hot_index_in.1, s32[1,1,2048]{2,1,0:T(1,128)} %hot_bag_in.1, ...), custom_call_target="tpu_custom_call" | custom-call | tf_op jit(solution)/shard_map/pallas_call | solution.py:610
  99.3 3.1 %shard_map.129 = (f32[128,256]{1,0:T(8,128)}, f32[1,256,512]{2,1,0:T(8,128)}, f32[1,128,512]{2,1,0:T(8,128)}, f32[1,1,1024,256]{3,2,1,0:T(8,128)}, f32[1,1,1024,128]{3,2,1,0:T(8,128)}) custom-call(f32[128,256]{1,0:T(8,128)} %get-tuple-element.10.refs_0_, f32[1,256,512]{2,1,0:T(8,128)} %get-tuple-element.11.refs_1_, ...), custom_call_target="tpu_custom_call" | custom-call | tf_op jit(solution)/shard_map/pallas_call | solution.py:635
